TPU v7x, 256 devices: a whole 4x4x8 slice. The times are simulated.
256 devices in a mesh: fv: 32 (over x_lo, z, core), tok: 8 (over y, x_hi).
Axes of the slice: x: 4 (x_hi: 2, x_lo: 2; x = x_hi * 2 + x_lo), y: 4, z: 8, core: 2. Of those that a mesh axis runs over, the one named last changes fastest.
Arguments:
- queries: bfloat16 [96, 1024, 1536], P('fv', 'tok'), may hold values from -6 to 6
- keys: bfloat16 [96, 1024, 1536], P('fv', 'tok'), may hold values from -6 to 6
- values: bfloat16 [96, 1024, 1536], P('fv', 'tok'), may hold values from -6 to 6
- adjacency: int32 [6, 2], replicated, may hold values from 0 to 5, as said below
Outputs:
- attended: bfloat16 [96, 1024, 1536], P('fv', 'tok')
Inputs may be any that keep to these rules, and one draw needn't show every extreme that they name: `adjacency`: row v holds the left and the right neighbour of camera v on one cycle through all 6 cameras.
All inputs are finite; a program needn't handle non-finite values.
Results may differ from a plain program's by a relative error of at most 0.0049.
Values may be sent and summed in bfloat16 or wider, within the bound.
A program may use at most 128 MiB of HBM per device.

v0:
```python
import jax
import jax.numpy as jnp
from jax import lax
from jax.sharding import PartitionSpec as P

VIEWS = 6
HEAD_DIM = 64
WIN = 128


def from_partner(x, axis, bit):
    return lax.ppermute(x, axis, [(i, i ^ 1 << bit) for i in range(lax.axis_size(axis))])


def with_halo(cells, sides, width):
    for axis, dim in sides:
        count = lax.axis_size(axis)
        ends = count - 1
        head = lax.slice_in_dim(cells, 0, width, axis=dim)
        tail = lax.slice_in_dim(cells, cells.shape[dim] - width, cells.shape[dim], axis=dim)
        cells = jnp.concatenate(
            [
                lax.ppermute(tail, axis, [(i, (i + 1) % count) for i in range(ends)]),
                cells,
                lax.ppermute(head, axis, [((i + 1) % count, i) for i in range(ends)]),
            ],
            axis=dim,
        )
    return cells


def arrange(parity, own_part, other_part):
    leading = jnp.where(parity == 0, own_part, other_part)
    trailing = jnp.where(parity == 0, other_part, own_part)
    return jnp.concatenate([leading, trailing], axis=1)


def view_attend(items, band_start, total_tokens):
    query_view, key_sets, value_sets = items
    band_rows, width_half = query_view.shape
    head_count = width_half // HEAD_DIM
    key_rows = key_sets.shape[1]
    query_heads = query_view.reshape(band_rows, head_count, HEAD_DIM)
    key_heads = key_sets.reshape(3, key_rows, head_count, HEAD_DIM)
    value_heads = value_sets.reshape(3, key_rows, head_count, HEAD_DIM)
    scores = jnp.einsum(
        "thd,skhd->htsk", query_heads, key_heads, preferred_element_type=jnp.float32
    ) * HEAD_DIM ** (-0.5)
    query_pos = band_start + jnp.arange(band_rows, dtype=jnp.int32)
    key_pos = band_start - WIN + jnp.arange(key_rows, dtype=jnp.int32)
    distance = query_pos[:, None] - key_pos[None, :]
    allowed = (
        (jnp.abs(distance) <= WIN) & (key_pos >= 0)[None, :] & (key_pos < total_tokens)[None, :]
    )
    scores = jnp.where(allowed[None, :, None, :], scores, -jnp.inf)
    row_max = jnp.max(scores, axis=(2, 3), keepdims=True)
    raised = jnp.exp(scores - row_max)
    denominator = jnp.sum(raised, axis=(2, 3), keepdims=True)
    weights = (raised / denominator).astype(jnp.bfloat16)
    mixed = jnp.einsum("htsk,skhd->thd", weights, value_heads, preferred_element_type=jnp.float32)
    return mixed.reshape(band_rows, width_half).astype(jnp.bfloat16)


def temporal_attend(gathered):
    _, pair_count, token_count, width_half = gathered.shape
    head_count = width_half // HEAD_DIM
    frame_count = pair_count // VIEWS
    shaped = gathered.reshape(3, frame_count, VIEWS, token_count, head_count, HEAD_DIM)
    scores = jnp.einsum(
        "fvthd,gvthd->vthfg", shaped[0], shaped[1], preferred_element_type=jnp.float32
    ) * HEAD_DIM ** (-0.5)
    row_max = jnp.max(scores, axis=-1, keepdims=True)
    raised = jnp.exp(scores - row_max)
    denominator = jnp.sum(raised, axis=-1, keepdims=True)
    weights = (raised / denominator).astype(jnp.bfloat16)
    mixed = jnp.einsum("vthfg,gvthd->fvthd", weights, shaped[2], preferred_element_type=jnp.float32)
    return mixed.reshape(pair_count, token_count, width_half).astype(jnp.bfloat16)


def body(queries, keys, values, adjacency):
    local_pairs, band_rows, width = queries.shape
    width_half = width // 2
    parity = lax.axis_index("fv") % 2
    band_start = lax.axis_index("tok") * band_rows
    total_tokens = band_rows * lax.axis_size("tok")
    stacked = jnp.stack([keys[:, :, :width_half], values[:, :, :width_half]])
    partner = from_partner(stacked, "fv", 0)
    frame_pairs = arrange(parity, stacked, partner)
    padded = with_halo(frame_pairs, (("tok", 2),), WIN)
    view_ids = jnp.arange(VIEWS, dtype=jnp.int32)
    local_views = parity * local_pairs + jnp.arange(local_pairs, dtype=jnp.int32)
    neighbours = adjacency[local_views]
    picked = jnp.stack([local_views, neighbours[:, 0], neighbours[:, 1]], axis=1)
    selector = (picked[:, :, None] == view_ids[None, None, :]).astype(jnp.bfloat16)
    chosen = jnp.einsum(
        "wsu,aukc->awskc", selector, padded, preferred_element_type=jnp.float32
    ).astype(jnp.bfloat16)
    cross_out = lax.map(
        lambda items: view_attend(items, band_start, total_tokens),
        (queries[:, :, :width_half], chosen[0], chosen[1]),
    )
    temporal_in = jnp.stack(
        [queries[:, :, width_half:], keys[:, :, width_half:], values[:, :, width_half:]]
    )
    gathered = lax.all_to_all(temporal_in, "fv", split_axis=2, concat_axis=1, tiled=True)
    temporal_mixed = temporal_attend(gathered)
    temporal_out = lax.all_to_all(temporal_mixed, "fv", split_axis=0, concat_axis=1, tiled=True)
    return jnp.concatenate([cross_out, temporal_out], axis=-1)


def solution(mesh):
    in_specs = (P("fv", "tok", None), P("fv", "tok", None), P("fv", "tok", None), P())
    out_specs = P("fv", "tok", None)
    return jax.shard_map(body, mesh=mesh, in_specs=in_specs, out_specs=out_specs, check_vma=False)
```

profile of v0, /device:TPU:1, one launch (start us, length us, event | category | flops | bytes accessed | tf_op | source)
XLA Modules:
  0.0 261.7 jit_solution(9532397097798608835)
XLA Ops:
  0.0 2.3 fusion.41
  5.6 2.7 %pad_maximum_fusion.1 = bf16[3,3,128,768]{3,1,0,2:T(4,128)(2,1)} fusion(bf16[1,3,128,768]{3,1,0,2:T(4,128)(2,1)S(1)} %get-tuple-element.146, bf16[1,3,128,768]{3,1,0,2:T(4,128)(2,1)S(1)} %get-tuple-element.147, bf16[1,3,128,768]{3,1,0,2:T(4,128)(2,1)S(1)} %bitcast.72), kind=kLoop, calls=%fused_computation.35 | loop fusion | flops 1769472 | bytes 3538944 | tf_op jit(solution)/shard_map/stack | solution.py:102
  8.3 11.1 %all-to-all-start = ((bf16[3,3,128,768]{3,1,0,2:T(4,128)(2,1)}), bf16[3,3,128,768]{3,1,0,2:T(4,128)(2,1)S(1)}, u32[]{:S(2)}, u32[]{:S(2)}) async-start(bf16[3,3,128,768]{3,1,0,2:T(4,128)(2,1)} %pad_maximum_fusion.1), calls=%async_computation | async-start | bytes 4718592 | tf_op jit(solution)/shard_map/all_to_all | solution.py:105
  24.2 3.0 %collective-permute-done = bf16[2,3,128,768]{3,2,1,0:T(8,128)(2,1)} collective-permute-done((bf16[2,3,128,768]{3,2,1,0:T(8,128)(2,1)}, bf16[2,3,128,768]{3,2,1,0:T(8,128)(2,1)}, u32[]{:S(2)}, u32[]{:S(2)}) %collective-permute-start) | collective-permute-done | bytes 1179680 | tf_op jit(solution)/shard_map/ppermute | solution.py:12
  27.1 3.5 %broadcast_select_fusion.1 = (bf16[2,3,128,768]{3,1,2,0:T(4,128)(2,1)S(1)}, bf16[2,3,128,768]{3,1,2,0:T(4,128)(2,1)S(1)}) fusion(pred[]{:T(512)S(6)} %eq.10, bf16[2,3,128,768]{3,2,1,0:T(8,128)(2,1)} %collective-permute-done, bf16[1,3,128,768]{3,1,2,0:T(4,128)(2,1)S(1)} %get-tuple-element.148, bf16[1,3,128,768]{3,1,2,0:T(4,128)(2,1)} %copy-done.1), kind=kLoop, calls=%fused_computation.43 | loop fusion | flops 1769472 | bytes 4718593 | tf_op jit(solution)/shard_map/jit(_where)/select_n | solution.py:33
  34.2 5.8 %collective-permute-start.1 = (bf16[2,6,128,768]{3,2,1,0:T(8,128)(2,1)}, bf16[2,6,128,768]{3,2,1,0:T(8,128)(2,1)}, u32[]{:S(2)}, u32[]{:S(2)}) collective-permute-start(bf16[2,6,128,768]{3,2,1,0:T(8,128)(2,1)} %copy.53), channel_id=1, source_target_pairs={{0,1},{1,2},{2,3},{3,4},{4,5},{5,6},{6,7},{8,9},{9,10},{10,11},{11... | collective-permute-start | bytes 7077896 | tf_op jit(solution)/shard_map/ppermute | solution.py:23
  42.4 32.2 %all-to-all-done = bf16[3,3,128,768]{3,1,0,2:T(4,128)(2,1)S(1)} async-done(((bf16[3,3,128,768]{3,1,0,2:T(4,128)(2,1)}), bf16[3,3,128,768]{3,1,0,2:T(4,128)(2,1)S(1)}, u32[]{:S(2)}, u32[]{:S(2)}) %all-to-all-start) | async-done | bytes 1769504 | tf_op jit(solution)/shard_map/all_to_all | solution.py:105
  80.2 3.1 %squeeze.22 = bf16[16,6,4,12,64]{4,3,2,1,0:T(8,128)(2,1)} reshape(bf16[1,32,3,4,768]{4,3,2,1,0:T(4,128)(2,1)} %get-tuple-element.135) | data formatting | bytes 1179648 | tf_op jit(solution)/shard_map/squeeze | solution.py:76
  84.7 10.0 %fusion.43 = (f32[6,4,12,16]{3,2,1,0:T(8,128)S(1)}, f32[6,4,12,16,16]{3,4,2,1,0:T(8,128)S(1)}) fusion(f32[6,4,12,16,16]{3,4,2,1,0:T(8,128)S(1)} %fusion.28), kind=kOutput, calls=%fused_computation.72 | output fusion | flops 294927 | bytes 608256 | tf_op jit(solution)/shard_map/sub | solution.py:73
  97.7 5.6 %all-to-all-start.1 = ((bf16[96,4,768]{2,1,0:T(4,128)(2,1)}), bf16[96,4,768]{2,1,0:T(4,128)(2,1)}, u32[]{:S(2)}, u32[]{:S(2)}) async-start(bf16[96,4,768]{2,1,0:T(4,128)(2,1)} %reshape.152), calls=%async_computation.1 | async-start | bytes 1179648 | tf_op jit(solution)/shard_map/all_to_all | solution.py:107
  104.0 3.0 %copy.55 = bf16[2,6,128,768]{3,1,2,0:T(8,128)(2,1)S(1)} copy(bf16[2,6,128,768]{3,2,1,0:T(8,128)(2,1)} %collective-permute-done.1) | data formatting | bytes 4718592 | tf_op jit(solution)/shard_map/ppermute | solution.py:23
  107.0 55.9 %collective-permute-done.2 = bf16[2,6,128,768]{3,2,1,0:T(8,128)(2,1)} collective-permute-done((bf16[2,6,128,768]{3,2,1,0:T(8,128)(2,1)}, bf16[2,6,128,768]{3,2,1,0:T(8,128)(2,1)}, u32[]{:S(2)}, u32[]{:S(2)}) %collective-permute-start.2) | collective-permute-done | bytes 2359328 | tf_op jit(solution)/shard_map/ppermute | solution.py:25
  162.8 3.0 %copy.56 = bf16[2,6,128,768]{3,1,2,0:T(8,128)(2,1)S(1)} copy(bf16[2,6,128,768]{3,2,1,0:T(8,128)(2,1)} %collective-permute-done.2) | data formatting | bytes 4718592 | tf_op jit(solution)/shard_map/ppermute | solution.py:25
  165.9 10.3 %convert_bitcast_fusion = bf16[2,3,3,384,768]{4,2,1,3,0:T(4,128)(2,1)} fusion(bf16[2,6,128,768]{3,1,2,0:T(8,128)(2,1)S(1)} %copy.56, bf16[2,3,128,768]{3,1,2,0:T(4,128)(2,1)S(1)} %copy-done.5, bf16[2,3,128,768]{3,1,2,0:T(4,128)(2,1)S(1)} %copy-done.3, bf16[2,6,128,768]{3,1,2,0:T(8,128)(2,1)S(1)} %copy.55, s32[3,3]{1,0:T(4,128)S(1)} %pad_add_fusion), kind=kOutput, calls=%fused_computation.24 | convolution fusion | flops 97321016 | bytes 17694756 | tf_op jit(solution)/shard_map/wsu,aukc->awskc/dot_general | solution.py:95
  176.2 14.6 %slice_bitcast_fusion = (bf16[3,3,384,768]{3,1,0,2:T(4,128)(2,1)}, bf16[3,3,384,768]{3,1,0,2:T(4,128)(2,1)}) fusion(bf16[2,3,3,384,768]{4,2,1,3,0:T(4,128)(2,1)} %convert_bitcast_fusion), kind=kLoop, calls=%fused_computation.32 | loop fusion | bytes 21233664 | tf_op jit(solution)/shard_map/squeeze | solution.py:100
  190.7 13.4 %copy.59 = bf16[3,3,384,768]{2,3,1,0:T(8,128)(2,1)} copy(bf16[3,3,384,768]{3,1,0,2:T(4,128)(2,1)} %get-tuple-element.132) | data formatting | bytes 10616832 | tf_op jit(solution)/shard_map/while | solution.py:98
  204.1 13.4 %copy.60 = bf16[3,3,384,768]{2,3,1,0:T(8,128)(2,1)} copy(bf16[3,3,384,768]{3,1,0,2:T(4,128)(2,1)} %get-tuple-element.131) | data formatting | bytes 10616832 | tf_op jit(solution)/shard_map/while | solution.py:98
  217.6 41.5 %while.12 = (s32[]{:T(128)}, bf16[3,128,768]{2,1,0:T(8,128)(2,1)}, bf16[3,3,384,768]{2,3,1,0:T(8,128)(2,1)}, s32[]{:T(128)}, s32[]{:T(128)}, /*index=5*/bf16[3,1...) while((s32[]{:T(128)}, bf16[3,128,768]{2,1,0:T(8,128)(2,1)}, ...), condition=%wide.region_3.4_spmd, body=%wide.region_0.3_spmd.sunk | while | flops 474561152 | bytes 34246788 | solution.py:98
  218.3 2.4 constant_dynamic-slice_fusion.5
  228.0 2.5 fusion.61
  232.2 2.4 constant_dynamic-slice_fusion.5
  241.9 2.5 fusion.61
  246.0 2.4 constant_dynamic-slice_fusion.5
  255.8 2.5 fusion.61
  (87 shorter events, 54.0 us)
Async XLA Ops:
  0.0 2.3 copy-start.7
  0.0 3.2 %copy-start.8 = (bf16[3,128,1536]{2,1,0:T(8,128)(2,1)S(1)}, bf16[3,128,1536]{2,1,0:T(8,128)(2,1)}, u32[]{:S(2)}) copy-start(bf16[3,128,1536]{2,1,0:T(8,128)(2,1)} %param.6) | copy-start | bytes 3538948
  8.3 66.3 %all-to-all-start = ((bf16[3,3,128,768]{3,1,0,2:T(4,128)(2,1)}), bf16[3,3,128,768]{3,1,0,2:T(4,128)(2,1)S(1)}, u32[]{:S(2)}, u32[]{:S(2)}) async-start(bf16[3,3,128,768]{3,1,0,2:T(4,128)(2,1)} %pad_maximum_fusion.1), calls=%async_computation | async-start | bytes 4718592 | tf_op jit(solution)/shard_map/all_to_all | solution.py:105
  21.6 2.3 copy-start.1
  23.9 3.2 %collective-permute-start = (bf16[2,3,128,768]{3,2,1,0:T(8,128)(2,1)}, bf16[2,3,128,768]{3,2,1,0:T(8,128)(2,1)}, u32[]{:S(2)}, u32[]{:S(2)}) collective-permute-start(bf16[2,3,128,768]{3,2,1,0:T(8,128)(2,1)} %copy.50), channel_id=1, source_target_pairs={{0,8},{8,0},{16,24},{24,16},{32,40},{40,32},{48,56},{56,48},{64,72... | collective-permute-start | bytes 3538952 | tf_op jit(solution)/shard_map/ppermute | solution.py:12
  30.6 1.6 copy-start.2
  30.6 1.6 copy-start.4
  32.3 9.2 %copy-start.10 = (s32[6,2]{0,1:T(2,128)S(1)}, s32[6,2]{0,1:T(2,128)}, u32[]{:S(2)}) copy-start(s32[6,2]{0,1:T(2,128)} %param.9) | copy-start | bytes 148
  34.2 69.8 %collective-permute-start.1 = (bf16[2,6,128,768]{3,2,1,0:T(8,128)(2,1)}, bf16[2,6,128,768]{3,2,1,0:T(8,128)(2,1)}, u32[]{:S(2)}, u32[]{:S(2)}) collective-permute-start(bf16[2,6,128,768]{3,2,1,0:T(8,128)(2,1)} %copy.53), channel_id=1, source_target_pairs={{0,1},{1,2},{2,3},{3,4},{4,5},{5,6},{6,7},{8,9},{9,10},{10,11},{11... | collective-permute-start | bytes 7077896 | tf_op jit(solution)/shard_map/ppermute | solution.py:23
  40.0 122.8 %collective-permute-start.2 = (bf16[2,6,128,768]{3,2,1,0:T(8,128)(2,1)}, bf16[2,6,128,768]{3,2,1,0:T(8,128)(2,1)}, u32[]{:S(2)}, u32[]{:S(2)}) collective-permute-start(bf16[2,6,128,768]{3,2,1,0:T(8,128)(2,1)} %copy.53), channel_id=1, source_target_pairs={{1,0},{2,1},{3,2},{4,3},{5,4},{6,5},{7,6},{9,8},{10,9},{11,10},{12... | collective-permute-start | bytes 7077896 | tf_op jit(solution)/shard_map/ppermute | solution.py:25
  84.7 10.1 %copy-start.6 = (bf16[16,6,4,12,64]{4,3,2,1,0:T(8,128)(2,1)S(1)}, bf16[16,6,4,12,64]{4,3,2,1,0:T(8,128)(2,1)}, u32[]{:S(2)}) copy-start(bf16[16,6,4,12,64]{4,3,2,1,0:T(8,128)(2,1)} %squeeze.22) | copy-start | bytes 1769476
  97.7 161.4 %all-to-all-start.1 = ((bf16[96,4,768]{2,1,0:T(4,128)(2,1)}), bf16[96,4,768]{2,1,0:T(4,128)(2,1)}, u32[]{:S(2)}, u32[]{:S(2)}) async-start(bf16[96,4,768]{2,1,0:T(4,128)(2,1)} %reshape.152), calls=%async_computation.1 | async-start | bytes 1179648 | tf_op jit(solution)/shard_map/all_to_all | solution.py:107
  107.0 58.9 %copy-start.3 = (bf16[2,3,128,768]{3,1,2,0:T(4,128)(2,1)S(1)}, bf16[2,3,128,768]{3,1,2,0:T(4,128)(2,1)}, u32[]{:S(2)}) copy-start(bf16[2,3,128,768]{3,1,2,0:T(4,128)(2,1)} %copy-done.2) | copy-start | bytes 3538948
  107.0 58.9 %copy-start.5 = (bf16[2,3,128,768]{3,1,2,0:T(4,128)(2,1)S(1)}, bf16[2,3,128,768]{3,1,2,0:T(4,128)(2,1)}, u32[]{:S(2)}) copy-start(bf16[2,3,128,768]{3,1,2,0:T(4,128)(2,1)} %copy-done.4) | copy-start | bytes 3538948
  224.1 2.2 copy-start
  237.9 2.2 copy-start
  251.8 2.2 copy-start
  259.1 1.5 copy-start.9
where the time goes:
time: 264 us; the launch traced here: 262 us
  waiting for transfers between devices  91.7 us (35%)
  local copies, waits for them, and re-layouts  91 us (34%)
  other arithmetic  27.8 us (11%)
  matrix products  26.7 us (10%)
  starting transfers between devices  24.1 us (9%)
    ppermute x1, waiting for transfers between devices, with_halo(): lax.ppermute(head, axis, [((i + 1) % count, i) for i in range(ends)])  55.9 us
    all_to_all x1, waiting for transfers between devices, body(): lax.all_to_all(temporal_in, 'fv', split_axis=2, concat_axis=1, tiled=True)  32.2 us
    while x2, local copies, waits for them, and re-layouts, body(): lax.map(lambda items: view_attend(items, band_start, total_tokens), (quer...  26.9 us
    dynamic_slice x9, local copies, waits for them, and re-layouts, body(): lax.map(lambda items: view_attend(items, band_start, total_tokens), (quer...  17.2 us
    squeeze x1, local copies, waits for them, and re-layouts, body(): chosen[0]  14.6 us
    all_to_all x1, starting transfers between devices, body(): lax.all_to_all(temporal_in, 'fv', split_axis=2, concat_axis=1, tiled=True)  11.1 us
    dot_general x1, matrix products, body(): jnp.einsum('wsu,aukc->awskc', selector, padded, preferred_element_type=jn...  10.3 us
    sub x1, other arithmetic, temporal_attend(): raised = jnp.exp(scores - row_max)  10 us
  transfers between devices with their start and end apart: 5, of which 4 were waited for; matrix products, arithmetic and copies ran while one was open for 51% of the time, Pallas kernels for 0%

commit v1 on v0

v1 whole, which is shorter than its diff:
```python
import jax
import jax.numpy as jnp
from jax import lax
from jax.experimental import pallas as pl
from jax.experimental.pallas import tpu as pltpu
from jax.sharding import PartitionSpec as P

MESH = pl.DeviceIdType.MESH
VIEWS = 6
CAMS = 3
HEAD_DIM = 64
FRAMES = 16
RING = 8
ROWS = 128
HALF = 768
GROUP = 16
COLS = 384
LANES = 128
FAR = -1e30
RATE = HEAD_DIM ** -0.5 * 1.4426950408889634
BF16 = jnp.bfloat16
F32 = jnp.float32


def lane_masks():
    lane = lax.broadcasted_iota(jnp.int32, (1, LANES), 1)
    low = (lane < HEAD_DIM).astype(F32)
    return low.astype(BF16), (1.0 - low).astype(BF16), lane < HEAD_DIM


def scores_of(q, k):
    return lax.dot_general(q, k, (((1,), (1,)), ((), ())), preferred_element_type=F32)


def mix(p, v):
    wide = jnp.concatenate([v, jnp.ones_like(v)], axis=1)
    return lax.dot_general(p, wide, (((1,), (0,)), ((), ())), preferred_element_type=F32)


def kernel(q, k, v, adj, out, qx, ko, vo, kx, vx, ky, vy, tr, ts, tout, co, part, bias_x, bias_y, bias_t,
           load_sem, own_sem, x_send, x_recv, xc_send, xc_recv, y_send, y_recv, yc_send, yc_recv,
           t_send, t_recv, r_send, r_recv, out_sem):
    fv = lax.axis_index("fv")
    tok = lax.axis_index("tok")
    core = fv % 2
    z = (fv // 2) % RING
    xl = fv // (2 * RING)
    xh = tok % 2
    y = tok // 2
    frame = fv // 2

    sibling = (fv + 1 - 2 * core, tok)
    across = (fv, tok + 1 - 2 * xh)
    step = 1 - 2 * xh
    up = (fv, ((y + step + 4) % 4) * 2 + xh)
    down = (fv, ((y - step + 4) % 4) * 2 + xh)

    def peer(dz, dx):
        pz = (z + dz) % RING
        px = (xl + dx) % 2
        return pz, px, (px * 2 * RING + pz * 2 + core, tok)

    peers = [(dz, 0) for dz in (1, 7, 2, 6, 3, 5, 4)] + [(dz, 1) for dz in (0, 1, 7, 2, 6, 3, 5, 4)]
    mine = pl.ds(core * CAMS, CAMS)
    cross_cols = pl.ds(0, HALF)

    local = [
        pltpu.make_async_copy(q.at[:, :, cross_cols], qx, load_sem.at[0]),
        pltpu.make_async_copy(k.at[:, :, cross_cols], ko.at[mine], own_sem.at[0]),
        pltpu.make_async_copy(v.at[:, :, cross_cols], vo.at[mine], own_sem.at[1]),
    ]
    for copy in local:
        copy.start()

    barrier = pltpu.get_barrier_semaphore()
    everyone = [sibling, across, up, down] + [peer(*d)[2] for d in peers]
    for device in everyone:
        pl.semaphore_signal(barrier, inc=1, device_id=device, device_id_type=MESH)
    pl.semaphore_wait(barrier, len(everyone))

    def remote(src, dst, send, recv, device):
        return pltpu.make_async_remote_copy(
            src_ref=src, dst_ref=dst, send_sem=send, recv_sem=recv, device_id=device, device_id_type=MESH)

    own_pairs = [
        remote(k.at[:, :, cross_cols], ko.at[mine], xc_send.at[6], own_sem.at[2], sibling),
        remote(v.at[:, :, cross_cols], vo.at[mine], xc_send.at[7], own_sem.at[3], sibling),
    ]
    for copy in own_pairs:
        copy.start()

    to_across = []
    for c in range(CAMS):
        for a, (src, dst) in enumerate(((k, kx), (v, vx))):
            to_across.append(remote(src.at[c, :, cross_cols], dst.at[core * CAMS + c],
                                    x_send.at[2 * c + a], x_recv.at[2 * c + a], across))
    for copy in to_across:
        copy.start()

    for a, src in enumerate((q, k, v)):
        for c in range(CAMS):
            pltpu.make_async_copy(
                src.at[c, pl.ds(pl.multiple_of(z * GROUP, GROUP), GROUP), pl.ds(pl.multiple_of(HALF + xl * COLS, LANES), COLS)],
                tr.at[c, a, frame], t_recv.at[c]).start()
    for c in range(CAMS):
        for d in peers:
            pz, px, device = peer(*d)
            for a, src in enumerate((q, k, v)):
                remote(
                    src.at[c, pl.ds(pl.multiple_of(pz * GROUP, GROUP), GROUP), pl.ds(pl.multiple_of(HALF + px * COLS, LANES), COLS)],
                    tr.at[c, a, frame], t_send.at[c], t_recv.at[c], device).start()

    row = lax.broadcasted_iota(jnp.int32, (ROWS, ROWS), 0)
    col = lax.broadcasted_iota(jnp.int32, (ROWS, ROWS), 1)
    sign = 1 - 2 * xh
    bias_x[...] = jnp.where((col - row) * sign <= 0, 0.0, FAR).astype(F32)
    inside = jnp.where(xh == 0, y, 3 - y) > 0
    edge = jnp.where(inside, 0, 2 * ROWS)
    bias_y[...] = jnp.where((col - row) * sign >= edge, 0.0, FAR).astype(F32)
    trow = lax.broadcasted_iota(jnp.int32, (FRAMES * GROUP, FRAMES * GROUP), 0)
    tcol = lax.broadcasted_iota(jnp.int32, (FRAMES * GROUP, FRAMES * GROUP), 1)
    bias_t[...] = jnp.where((trow - tcol) % GROUP == 0, 0.0, FAR).astype(F32)

    low, high, is_low = lane_masks()

    def block(kbuf, vbuf, bias, w, cols):
        qv = qx[w, :, cols]
        both = jnp.concatenate([qv * low, qv * high], axis=0)
        view = core * CAMS + w
        cams = (view, adj[view, 0], adj[view, 1])
        s = scores_of(both, jnp.concatenate([kbuf[c, :, cols] for c in cams], axis=0))
        if bias is not None:
            b = bias[...]
            b = jnp.concatenate([b, b, b], axis=1)
            s = s + jnp.concatenate([b, b], axis=0)
        m = jnp.max(s, axis=1, keepdims=True)
        p = jnp.exp2((s - m) * RATE).astype(BF16)
        o = mix(p, jnp.concatenate([vbuf[c, :, cols] for c in cams], axis=0))
        top = jnp.where(is_low, m[:ROWS], m[ROWS:])
        total = jnp.where(is_low, o[:ROWS, LANES:], o[ROWS:, LANES:])
        acc = jnp.where(is_low, o[:ROWS, :LANES], o[ROWS:, :LANES])
        return top, total, acc

    def pass_over(kbuf, vbuf, bias, slot):
        def one(p, _):
            cols = pl.ds(pl.multiple_of(p * LANES, LANES), LANES)
            for w in range(CAMS):
                res = block(kbuf, vbuf, bias, w, cols)
                if slot < 2:
                    for i in range(3):
                        part[slot, i, w, p] = res[i]
                else:
                    tops = [part[0, 0, w, p], part[1, 0, w, p], res[0]]
                    top = jnp.maximum(jnp.maximum(tops[0], tops[1]), tops[2])
                    e = [jnp.exp2((t - top) * RATE) for t in tops]
                    total = part[0, 1, w, p] * e[0] + part[1, 1, w, p] * e[1] + res[1] * e[2]
                    acc = part[0, 2, w, p] * e[0] + part[1, 2, w, p] * e[1] + res[2] * e[2]
                    co[w, :, cols] = (acc / total).astype(BF16)
            return 0
        lax.fori_loop(0, HALF // LANES, one, 0)

    for copy in local:
        copy.wait()
    for copy in own_pairs:
        copy.wait()
    pass_over(ko, vo, None, 0)

    forwards, pairs_x = [], []
    for c in range(CAMS):
        for a, (xb, yb) in enumerate(((kx, ky), (vx, vy))):
            i = 2 * c + a
            to_across[i].wait_recv()
            slot = core * CAMS + c
            f = remote(xb.at[slot], yb.at[slot], y_send.at[i], y_recv.at[i], up)
            f.start()
            forwards.append(f)
            g = remote(xb.at[slot], xb.at[slot], xc_send.at[i], xc_recv.at[i], sibling)
            g.start()
            pairs_x.append(g)
    for g in pairs_x:
        g.wait_recv()
    pass_over(kx, vx, bias_x, 1)

    pairs_y = []
    for c in range(CAMS):
        for a, yb in enumerate((ky, vy)):
            i = 2 * c + a
            forwards[i].wait_recv()
            slot = core * CAMS + c
            g = remote(yb.at[slot], yb.at[slot], yc_send.at[i], yc_recv.at[i], sibling)
            g.start()
            pairs_y.append(g)

    def temporal(c):
        pltpu.make_async_copy(tr.at[c], tr.at[c], t_recv.at[c]).wait()

        def one(p, _):
            cols = pl.ds(pl.multiple_of(p * LANES, LANES), LANES)
            flat = FRAMES * GROUP
            qt, kt, vt = (tr[c, a, :, :, cols].reshape(flat, LANES) for a in range(3))
            res = []
            for mask in (low, high):
                s = scores_of(qt * mask, kt) + bias_t[...]
                m = jnp.max(s, axis=1, keepdims=True)
                o = mix(jnp.exp2((s - m) * RATE).astype(BF16), vt)
                res.append(o[:, :LANES] / o[:, LANES:])
            o = jnp.where(is_low, res[0], res[1]).astype(BF16)
            ts[c, :, :, cols] = o.reshape(FRAMES, GROUP, LANES)
            return 0
        lax.fori_loop(0, COLS // LANES, one, 0)
        place = (c, pl.ds(pl.multiple_of(z * GROUP, GROUP), GROUP), pl.ds(pl.multiple_of(xl * COLS, LANES), COLS))
        pltpu.make_async_copy(ts.at[c, frame], tout.at[place], r_recv.at[c]).start()
        for d in peers:
            pz, px, device = peer(*d)
            remote(ts.at[c, px * RING + pz], tout.at[place], r_send.at[c], r_recv.at[c], device).start()

    for c in range(CAMS):
        temporal(c)

    for g in pairs_y:
        g.wait_recv()
    pass_over(ky, vy, bias_y, 2)
    last = [pltpu.make_async_copy(co, out.at[:, :, cross_cols], out_sem.at[CAMS])]
    last[0].start()
    for c in range(CAMS):
        pltpu.make_async_copy(tout.at[c], tout.at[c], r_recv.at[c]).wait()
        copy = pltpu.make_async_copy(tout.at[c], out.at[c, :, pl.ds(HALF, HALF)], out_sem.at[c])
        copy.start()
        last.append(copy)

    for copy in to_across + forwards + pairs_x + pairs_y:
        copy.wait_send()
    for c in range(CAMS):
        sent = tr.at[c, :, pl.ds(0, FRAMES - 1)]
        pltpu.make_async_copy(sent, sent, t_send.at[c]).wait()
        sent = ts.at[c, pl.ds(0, FRAMES - 1)]
        pltpu.make_async_copy(sent, sent, r_send.at[c]).wait()
    for copy in last:
        copy.wait()


def body(queries, keys, values, adjacency):
    dma = pltpu.SemaphoreType.DMA
    any_spec = pl.BlockSpec(memory_space=pl.ANY)
    six = pltpu.VMEM((VIEWS, ROWS, HALF), BF16)
    three = pltpu.VMEM((CAMS, ROWS, HALF), BF16)
    flat = FRAMES * GROUP
    return pl.pallas_call(
        kernel,
        out_shape=jax.ShapeDtypeStruct(queries.shape, BF16),
        in_specs=[any_spec] * 3 + [pl.BlockSpec(memory_space=pltpu.SMEM)],
        out_specs=any_spec,
        scratch_shapes=[
            three, six, six, six, six, six, six,
            pltpu.VMEM((CAMS, 3, FRAMES, GROUP, COLS), BF16),
            pltpu.VMEM((CAMS, FRAMES, GROUP, COLS), BF16),
            three, three,
            pltpu.VMEM((2, 3, CAMS, HALF // LANES, ROWS, LANES), F32),
            pltpu.VMEM((ROWS, ROWS), F32),
            pltpu.VMEM((ROWS, ROWS), F32),
            pltpu.VMEM((flat, flat), F32),
            dma((1,)), dma((4,)), dma((6,)), dma((6,)), dma((8,)), dma((6,)), dma((6,)), dma((6,)), dma((6,)), dma((6,)),
            dma((3,)), dma((3,)), dma((3,)), dma((3,)), dma((4,)),
        ],
        compiler_params=pltpu.CompilerParams(
            collective_id=0, has_side_effects=True, vmem_limit_bytes=48 << 20),
        cost_estimate=pl.CostEstimate(flops=3_000_000_000, bytes_accessed=5_000_000, transcendentals=7_000_000),
        name="views_and_frames",
    )(queries, keys, values, adjacency)


def solution(mesh):
    in_specs = (P("fv", "tok", None), P("fv", "tok", None), P("fv", "tok", None), P())
    return jax.shard_map(body, mesh=mesh, in_specs=in_specs, out_specs=P("fv", "tok", None), check_vma=False)
```

time: 264 us -> 85.8 us (0.33)
  waiting for transfers between devices: 91.7 us -> 0 us
  local copies, waits for them, and re-layouts: 91 us -> 5.59 us
  Pallas kernels: 0 us -> 80 us
  other arithmetic: 27.8 us -> 0 us
  matrix products: 26.7 us -> 0 us
  starting transfers between devices: 24.1 us -> 0 us
    pallas_call x0 -> x1, Pallas kernels: none -> 80 us  [body(): pl.pallas_call(kernel, out_shape=jax.ShapeDtypeStruct(queries.shape, BF16...]
    ppermute x3 -> x0, waiting for transfers between devices: 59.5 us -> none  [the longest x1 55.9 us: with_halo(): lax.ppermute(head, axis, [((i + 1) % count, i) for i in range(ends)])]
    all_to_all x2 -> x0, waiting for transfers between devices: 32.2 us -> none  [the longest x1 32.2 us: body(): lax.all_to_all(temporal_in, 'fv', split_axis=2, concat_axis=1, tiled=True)]
    while x8 -> x0, local copies, waits for them, and re-layouts: 26.9 us -> none  [the longest x2 26.9 us: body(): lax.map(lambda items: view_attend(items, band_start, total_tokens), (quer...]
    dot_general x9 -> x0, matrix products: 26.7 us -> none  [the longest x1 10.3 us: body(): jnp.einsum('wsu,aukc->awskc', selector, padded, preferred_element_type=jn...]
    squeeze x4 -> x0, local copies, waits for them, and re-layouts: 20.8 us -> none  [the longest x1 14.6 us: body(): chosen[0]]
    dynamic_slice x9 -> x0, local copies, waits for them, and re-layouts: 17.2 us -> none  [body(): lax.map(lambda items: view_attend(items, band_start, total_tokens), (quer...]
    all_to_all x2 -> x0, starting transfers between devices: 16.6 us -> none  [the longest x1 11.1 us: body(): lax.all_to_all(temporal_in, 'fv', split_axis=2, concat_axis=1, tiled=True)]
  transfers between devices with their start and end apart: 5 -> 0, of which waited for: 4 -> 0; matrix products, arithmetic and copies ran while one was open for 51% -> 0% of each run, Pallas kernels for 0% -> 0%
where the time goes in v1:
time: 85.8 us; the launch traced here: 85.6 us
  Pallas kernels  80 us (93%)
  local copies, waits for them, and re-layouts  5.59 us (7%)
    pallas_call x1, Pallas kernels, body(): pl.pallas_call(kernel, out_shape=jax.ShapeDtypeStruct(queries.shape, BF16...  80 us
    unnamed x8, local copies, waits for them, and re-layouts  5.59 us

profile of v1, /device:TPU:1, one launch (start us, length us, event | category | flops | bytes accessed | tf_op | source)
XLA Modules:
  0.0 85.6 jit_solution(12320160890667739876)
XLA Ops:
  0.0 0.8 copy.5.adj
  0.8 0.0 copy-start
  0.8 1.3 %copy-done = bf16[3,128,1536]{2,1,0:T(8,128)(2,1)S(1)} copy-done((bf16[3,128,1536]{2,1,0:T(8,128)(2,1)S(1)}, bf16[3,128,1536]{2,1,0:T(8,128)(2,1)}, u32[]{:S(2)}) %copy-start) | copy-done | bytes 1179672
  2.0 0.0 copy-start.1
  2.0 1.3 %copy-done.1 = bf16[3,128,1536]{2,1,0:T(8,128)(2,1)S(1)} copy-done((bf16[3,128,1536]{2,1,0:T(8,128)(2,1)S(1)}, bf16[3,128,1536]{2,1,0:T(8,128)(2,1)}, u32[]{:S(2)}) %copy-start.1) | copy-done | bytes 1179672
  3.3 0.0 copy-start.2
  3.3 1.3 %copy-done.2 = bf16[3,128,1536]{2,1,0:T(8,128)(2,1)S(1)} copy-done((bf16[3,128,1536]{2,1,0:T(8,128)(2,1)S(1)}, bf16[3,128,1536]{2,1,0:T(8,128)(2,1)}, u32[]{:S(2)}) %copy-start.2) | copy-done | bytes 1179672
  4.6 80.0 %views_and_frames.1 = bf16[3,128,1536]{2,1,0:T(8,128)(2,1)S(1)} custom-call(bf16[3,128,1536]{2,1,0:T(8,128)(2,1)S(1)} %copy-done, bf16[3,128,1536]{2,1,0:T(8,128)(2,1)S(1)} %copy-done.1, bf16[3,128,1536]{2,1,0:T(8,128)(2,1)S(1)} %copy-done.2, s32[6,2]{1,0:T(8,128)S(1)} %copy.5.adj), custom_call_target="tpu_custom_call" | custom-call | flops 3000000000 | bytes 5000000 | tf_op jit(solution)/shard_map/views_and_frames/pallas_call | solution.py:248
  84.6 1.0 %copy.7 = bf16[3,128,1536]{2,1,0:T(8,128)(2,1)} copy(bf16[3,128,1536]{2,1,0:T(8,128)(2,1)S(1)} %views_and_frames.1) | data formatting | bytes 2359296
Async XLA Ops:
  0.8 1.3 %copy-start = (bf16[3,128,1536]{2,1,0:T(8,128)(2,1)S(1)}, bf16[3,128,1536]{2,1,0:T(8,128)(2,1)}, u32[]{:S(2)}) copy-start(bf16[3,128,1536]{2,1,0:T(8,128)(2,1)} %q.1) | copy-start | bytes 3538948
  2.0 1.3 %copy-start.1 = (bf16[3,128,1536]{2,1,0:T(8,128)(2,1)S(1)}, bf16[3,128,1536]{2,1,0:T(8,128)(2,1)}, u32[]{:S(2)}) copy-start(bf16[3,128,1536]{2,1,0:T(8,128)(2,1)} %k.1) | copy-start | bytes 3538948
  3.3 1.3 %copy-start.2 = (bf16[3,128,1536]{2,1,0:T(8,128)(2,1)S(1)}, bf16[3,128,1536]{2,1,0:T(8,128)(2,1)}, u32[]{:S(2)}) copy-start(bf16[3,128,1536]{2,1,0:T(8,128)(2,1)} %v.1) | copy-start | bytes 3538948

commit v2 on v1

v2 whole, which is shorter than its diff:
```python
import jax
import jax.numpy as jnp
from jax import lax
from jax.experimental import pallas as pl
from jax.experimental.pallas import tpu as pltpu
from jax.sharding import PartitionSpec as P

MESH = pl.DeviceIdType.MESH
VIEWS = 6
CAMS = 3
HEAD_DIM = 64
FRAMES = 16
RING = 8
ROWS = 128
HALF = 768
GROUP = 16
COLS = 384
LANES = 128
FAR = -1e30
RATE = HEAD_DIM ** -0.5 * 1.4426950408889634
BF16 = jnp.bfloat16
F32 = jnp.float32
GROUPS = 6
DIRECT = (2,)


def lane_masks():
    lane = lax.broadcasted_iota(jnp.int32, (1, LANES), 1)
    low = (lane < HEAD_DIM).astype(F32)
    return low.astype(BF16), (1.0 - low).astype(BF16), lane < HEAD_DIM


def scores_of(q, k):
    return lax.dot_general(q, k, (((1,), (1,)), ((), ())), preferred_element_type=F32)


def mix(p, v):
    wide = jnp.concatenate([v, jnp.ones_like(v)], axis=1)
    return lax.dot_general(p, wide, (((1,), (0,)), ((), ())), preferred_element_type=F32)


def kernel(q, k, v, adj, out_c, out_t, qx, ko, vo, kx, vx, ky, vy, tr, ts, co, lo, rb, part, bias_x, bias_y, bias_t,
           load_sem, own_sem, own_send, x_send, x_recv, xc_send, xc_recv, y_send, y_recv, yc_send, yc_recv,
           t_send, t_recv, r_send, r_recv, lo_send, lo_recv, rb_recv, rx_send, rx_recv, out_sem):
    fv = lax.axis_index("fv")
    tok = lax.axis_index("tok")
    core = fv % 2
    z = (fv // 2) % RING
    xl = fv // (2 * RING)
    xh = tok % 2
    y = tok // 2
    frame = fv // 2

    sibling = (fv + 1 - 2 * core, tok)
    across = (fv, tok + 1 - 2 * xh)
    step = 1 - 2 * xh
    up = (fv, ((y + step + 4) % 4) * 2 + xh)
    down = (fv, ((y - step + 4) % 4) * 2 + xh)

    beside = ((1 - xl) * 2 * RING + z * 2 + core, tok)
    other_frame = (1 - xl) * RING + z

    def peer(dz):
        pz = (z + dz) % RING
        return pz, (xl * 2 * RING + pz * 2 + core, tok)

    peers = (1, 7, 2, 6, 3, 5, 4)
    mine = pl.ds(core * CAMS, CAMS)
    cross_cols = pl.ds(0, HALF)

    local = [
        pltpu.make_async_copy(q.at[:, :, cross_cols], qx, load_sem.at[0]),
        pltpu.make_async_copy(k.at[:, :, cross_cols], ko.at[mine], own_sem.at[0]),
        pltpu.make_async_copy(v.at[:, :, cross_cols], vo.at[mine], own_sem.at[1]),
    ]

    def diagonal(dz):
        pz = (z + dz) % RING
        return pz, ((1 - xl) * 2 * RING + pz * 2 + core, tok)

    barrier = pltpu.get_barrier_semaphore()
    everyone = [sibling, across, beside, up, down] + [peer(d)[1] for d in peers]
    if DIRECT:
        everyone += [diagonal(d)[1] for d in peers]
    for device in everyone:
        pl.semaphore_signal(barrier, inc=1, device_id=device, device_id_type=MESH)
    pl.semaphore_wait(barrier, len(everyone))

    def remote(src, dst, send, recv, device):
        return pltpu.make_async_remote_copy(
            src_ref=src, dst_ref=dst, send_sem=send, recv_sem=recv, device_id=device, device_id_type=MESH)

    own_pairs = [
        remote(k.at[:, :, cross_cols], ko.at[mine], own_send.at[0], own_sem.at[2], sibling),
        remote(v.at[:, :, cross_cols], vo.at[mine], own_send.at[1], own_sem.at[3], sibling),
    ]

    def start_own():
        for copy in local + own_pairs:
            copy.start()

    width = HALF // GROUPS
    to_across = []
    for g in range(GROUPS):
        for a, (src, dst) in enumerate(((k, kx), (v, vx))):
            to_across.append(remote(src.at[:, :, pl.ds(g * width, width)], dst[g].at[mine],
                                    x_send.at[g, a], x_recv.at[g, a], across))

    def across_send(c):
        for copy in to_across[2 * c:2 * c + 2]:
            copy.start()

    def rows_of(pz):
        return pl.ds(pl.multiple_of(pz * GROUP, GROUP), GROUP)

    def half_of(px, start=0):
        return pl.ds(pl.multiple_of(start + px * COLS, LANES), COLS)

    to_beside = [
        [remote(src.at[c, :, half_of(1 - xl, HALF)], lo.at[c, a], lo_send.at[c, a], lo_recv.at[c, a], beside)
         for a, src in enumerate((q, k, v))] for c in range(CAMS)]

    def beside_send(c):
        for copy in to_beside[c]:
            copy.start()

    def own_send(c):
        for a, src in enumerate((q, k, v)):
            pltpu.make_async_copy(src.at[c, rows_of(z), half_of(xl, HALF)], tr.at[c, a, frame], t_recv.at[c]).start()
        for d in peers:
            pz, device = peer(d)
            for a, src in enumerate((q, k, v)):
                remote(src.at[c, rows_of(pz), half_of(xl, HALF)], tr.at[c, a, frame],
                       t_send.at[c], t_recv.at[c], device).start()

    def other_send(c):
        for a in range(3):
            to_beside[c][a].wait_recv()
            pltpu.make_async_copy(lo.at[c, a, rows_of(z)], tr.at[c, a, other_frame], t_recv.at[c]).start()
            for d in peers:
                pz, device = peer(d)
                remote(lo.at[c, a, rows_of(pz)], tr.at[c, a, other_frame],
                       t_send.at[c], t_recv.at[c], device).start()

    row = lax.broadcasted_iota(jnp.int32, (ROWS, ROWS), 0)
    col = lax.broadcasted_iota(jnp.int32, (ROWS, ROWS), 1)
    sign = 1 - 2 * xh
    bias_x[...] = jnp.where((col - row) * sign <= 0, 0.0, FAR).astype(F32)
    inside = jnp.where(xh == 0, y, 3 - y) > 0
    edge = jnp.where(inside, 0, 2 * ROWS)
    bias_y[...] = jnp.where((col - row) * sign >= edge, 0.0, FAR).astype(F32)
    trow = lax.broadcasted_iota(jnp.int32, (FRAMES * GROUP, FRAMES * GROUP), 0)
    tcol = lax.broadcasted_iota(jnp.int32, (FRAMES * GROUP, FRAMES * GROUP), 1)
    bias_t[...] = jnp.where((trow - tcol) % GROUP == 0, 0.0, FAR).astype(F32)

    low, high, is_low = lane_masks()

    def block(kbuf, vbuf, bias, w, cols, inner):
        qv = qx[w, :, cols]
        both = jnp.concatenate([qv * low, qv * high], axis=0)
        view = core * CAMS + w
        cams = (view, adj[0, view], adj[1, view])
        s = scores_of(both, jnp.concatenate([kbuf[c, :, inner] for c in cams], axis=0))
        if bias is not None:
            b = bias[...]
            b = jnp.concatenate([b, b, b], axis=1)
            s = s + jnp.concatenate([b, b], axis=0)
        m = jnp.max(s, axis=1, keepdims=True)
        p = jnp.exp2((s - m) * RATE).astype(BF16)
        o = mix(p, jnp.concatenate([vbuf[c, :, inner] for c in cams], axis=0))
        top = jnp.where(is_low, m[:ROWS], m[ROWS:])
        total = jnp.where(is_low, o[:ROWS, LANES:], o[ROWS:, LANES:])
        acc = jnp.where(is_low, o[:ROWS, :LANES], o[ROWS:, :LANES])
        return top, total, acc

    def pass_over(kbuf, vbuf, bias, slot, g=0, groups=1):
        per = HALF // LANES // groups

        def one(i, _):
            p = g * per + i
            cols = pl.ds(pl.multiple_of(p * LANES, LANES), LANES)
            inner = pl.ds(pl.multiple_of(i * LANES, LANES), LANES)
            found = [block(kbuf, vbuf, bias, w, cols, inner) for w in range(CAMS)]
            for w, res in enumerate(found):
                if slot < 2:
                    for i in range(3):
                        part[slot, i, w, p] = res[i]
                else:
                    tops = [part[0, 0, w, p], part[1, 0, w, p], res[0]]
                    top = jnp.maximum(jnp.maximum(tops[0], tops[1]), tops[2])
                    e = [jnp.exp2((t - top) * RATE) for t in tops]
                    total = part[0, 1, w, p] * e[0] + part[1, 1, w, p] * e[1] + res[1] * e[2]
                    acc = part[0, 2, w, p] * e[0] + part[1, 2, w, p] * e[1] + res[2] * e[2]
                    co[w, :, cols] = (acc / total).astype(BF16)
            return 0
        if per == 1:
            one(0, 0)
        else:
            lax.fori_loop(0, per, one, 0)

    def temporal(c):
        pltpu.make_async_copy(tr.at[c], tr.at[c], t_recv.at[c]).wait()

        def one(p, _):
            cols = pl.ds(pl.multiple_of(p * LANES, LANES), LANES)
            flat = FRAMES * GROUP
            qt, kt, vt = (tr[c, a, :, :, cols].reshape(flat, LANES) for a in range(3))
            res = []
            for mask in (low, high):
                s = scores_of(qt * mask, kt) + bias_t[...]
                m = jnp.max(s, axis=1, keepdims=True)
                o = mix(jnp.exp2((s - m) * RATE).astype(BF16), vt)
                res.append(o[:, :LANES] / o[:, LANES:])
            o = jnp.where(is_low, res[0], res[1]).astype(BF16)
            ts[c, :, :, cols] = o.reshape(FRAMES, GROUP, LANES)
            return 0
        lax.fori_loop(0, COLS // LANES, one, 0)
        place = (c, rows_of(z), half_of(xl))
        pltpu.make_async_copy(ts.at[c, frame], out_t.at[place], r_recv.at[c]).start()
        if c in DIRECT:
            for d in peers:
                pz, device = diagonal(d)
                remote(ts.at[c, (1 - xl) * RING + pz], out_t.at[place], r_send.at[c], rx_recv.at[c], device).start()
                pz, device = peer(d)
                remote(ts.at[c, xl * RING + pz], out_t.at[place], r_send.at[c], r_recv.at[c], device).start()
            remote(ts.at[c, other_frame], out_t.at[place], rx_send.at[c], rx_recv.at[c], beside).start()
            return
        pltpu.make_async_copy(ts.at[c, other_frame], rb.at[c, rows_of(z)], rb_recv.at[c]).start()
        for d in peers:
            pz, device = peer(d)
            remote(ts.at[c, xl * RING + pz], out_t.at[place], r_send.at[c], r_recv.at[c], device).start()
            remote(ts.at[c, (1 - xl) * RING + pz], rb.at[c, rows_of(z)], r_send.at[c], rb_recv.at[c], device).start()

    back = [remote(rb.at[c], out_t.at[c, :, half_of(xl)], rx_send.at[c], rx_recv.at[c], beside) for c in range(CAMS)]

    def relay(c):
        if c in DIRECT:
            return
        pltpu.make_async_copy(rb.at[c], rb.at[c], rb_recv.at[c]).wait()
        back[c].start()

    def pass_own():
        for copy in local:
            copy.wait()
        for copy in own_pairs:
            copy.wait()
        pass_over(ko, vo, None, 0)

    forwards, pairs_x, pairs_y = {}, {}, {}

    def forward_x(g):
        for a, (xb, yb) in enumerate(((kx, ky), (vx, vy))):
            to_across[2 * g + a].wait_recv()
            forwards[g, a] = remote(xb[g].at[mine], yb[g].at[mine], y_send.at[g, a], y_recv.at[g, a], up)
            forwards[g, a].start()
            pairs_x[g, a] = remote(xb[g].at[mine], xb[g].at[mine], xc_send.at[g, a], xc_recv.at[g, a], sibling)
            pairs_x[g, a].start()

    def pass_x(g):
        for a in range(2):
            pairs_x[g, a].wait_recv()
        pass_over(kx[g], vx[g], bias_x, 1, g, GROUPS)

    def forward_y(g):
        for a, yb in enumerate((ky, vy)):
            forwards[g, a].wait_recv()
            pairs_y[g, a] = remote(yb[g].at[mine], yb[g].at[mine], yc_send.at[g, a], yc_recv.at[g, a], sibling)
            pairs_y[g, a].start()

    def pass_y(g):
        for a in range(2):
            pairs_y[g, a].wait_recv()
        pass_over(ky[g], vy[g], bias_y, 2, g, GROUPS)
        here = (slice(None), slice(None), pl.ds(g * width, width))
        last.append(pltpu.make_async_copy(co.at[here], out_c.at[here], out_sem.at[g]))
        last[-1].start()

    last = []
    beside_send(0)
    own_send(0)
    start_own()
    beside_send(1)
    own_send(1)
    beside_send(2)
    own_send(2)
    pass_own()
    other_send(0)
    across_send(0)
    across_send(1)
    other_send(1)
    across_send(2)
    across_send(3)
    other_send(2)
    across_send(4)
    across_send(5)
    forward_x(0)
    forward_x(1)
    temporal(0)
    pass_x(0)
    pass_x(1)
    forward_y(0)
    forward_x(2)
    forward_y(1)
    pass_y(0)
    temporal(1)
    forward_x(3)
    pass_x(2)
    pass_x(3)
    forward_y(2)
    pass_y(1)
    forward_x(4)
    pass_y(2)
    temporal(2)
    pass_x(4)
    forward_y(3)
    forward_x(5)
    pass_x(5)
    pass_y(3)
    relay(0)
    forward_y(4)
    pass_y(4)
    relay(1)
    forward_y(5)
    pass_y(5)

    for copy in to_across + sum(to_beside, []) + [*forwards.values(), *pairs_x.values(), *pairs_y.values()]:
        copy.wait_send()
    for c in range(CAMS):
        sent = tr.at[c, :, pl.ds(0, FRAMES - 2)]
        pltpu.make_async_copy(sent, sent, t_send.at[c]).wait()
        sent = ts.at[c, pl.ds(0, FRAMES - 2)]
        pltpu.make_async_copy(sent, sent, r_send.at[c]).wait()
        if c in DIRECT:
            pltpu.make_async_copy(ts.at[c, 0], ts.at[c, 0], rx_send.at[c]).wait()
        else:
            back[c].wait_send()
        for half, sem in ((xl, r_recv), (1 - xl, rx_recv)):
            here = out_t.at[c, :, half_of(half)]
            pltpu.make_async_copy(here, here, sem.at[c]).wait()
    for copy in last:
        copy.wait()


def body(queries, keys, values, adjacency):
    dma = pltpu.SemaphoreType.DMA
    any_spec = pl.BlockSpec(memory_space=pltpu.HBM)
    six = pltpu.VMEM((VIEWS, ROWS, HALF), BF16)
    three = pltpu.VMEM((CAMS, ROWS, HALF), BF16)
    flat = FRAMES * GROUP
    cross, temporal = pl.pallas_call(
        kernel,
        out_shape=[jax.ShapeDtypeStruct((CAMS, ROWS, HALF), BF16)] * 2,
        in_specs=[any_spec] * 3 + [pl.BlockSpec(memory_space=pltpu.SMEM)],
        out_specs=[any_spec] * 2,
        scratch_shapes=[
            three, six, six, *[[pltpu.VMEM((VIEWS, ROWS, HALF // GROUPS), BF16)] * GROUPS] * 4,
            pltpu.VMEM((CAMS, 3, FRAMES, GROUP, COLS), BF16),
            pltpu.VMEM((CAMS, FRAMES, GROUP, COLS), BF16),
            three,
            pltpu.VMEM((CAMS, 3, ROWS, COLS), BF16),
            pltpu.VMEM((CAMS, ROWS, COLS), BF16),
            pltpu.VMEM((2, 3, CAMS, HALF // LANES, ROWS, LANES), F32),
            pltpu.VMEM((ROWS, ROWS), F32),
            pltpu.VMEM((ROWS, ROWS), F32),
            pltpu.VMEM((flat, flat), F32),
            dma((1,)), dma((4,)), dma((2,)), *[dma((GROUPS, 2))] * 8,
            dma((3,)), dma((3,)), dma((3,)), dma((3,)),
            dma((3, 3)), dma((3, 3)), dma((3,)), dma((3,)), dma((3,)), dma((GROUPS,)),
        ],
        compiler_params=pltpu.CompilerParams(
            collective_id=0, has_side_effects=True, vmem_limit_bytes=60 << 20),
        cost_estimate=pl.CostEstimate(flops=3_000_000_000, bytes_accessed=5_000_000, transcendentals=7_000_000),
        name="views_and_frames",
    )(queries, keys, values, adjacency.T)
    return jnp.concatenate([cross, temporal], axis=-1)


def solution(mesh):
    in_specs = (P("fv", "tok", None), P("fv", "tok", None), P("fv", "tok", None), P())
    return jax.shard_map(body, mesh=mesh, in_specs=in_specs, out_specs=P("fv", "tok", None), check_vma=False)
```

time: 85.8 us -> 73 us (0.85)
  Pallas kernels: 80 us -> 70.5 us
  local copies, waits for them, and re-layouts: 5.59 us -> 0 us
  other arithmetic: 0 us -> 2.34 us
    pallas_call x1, Pallas kernels: 80 us -> 70.5 us  [body(): pl.pallas_call(kernel, out_shape=[jax.ShapeDtypeStruct((CAMS, ROWS, HALF)...]
    unnamed x8 -> x0, local copies, waits for them, and re-layouts: 5.59 us -> none
    concatenate x0 -> x1, other arithmetic: none -> 2.34 us  [body(): return jnp.concatenate([cross, temporal], axis=-1)]
where the time goes in v2:
time: 73 us; the launch traced here: 72.9 us
  Pallas kernels  70.5 us (97%)
  other arithmetic  2.34 us (3%)
    pallas_call x1, Pallas kernels, body(): pl.pallas_call(kernel, out_shape=[jax.ShapeDtypeStruct((CAMS, ROWS, HALF)...  70.5 us
    concatenate x1, other arithmetic, body(): return jnp.concatenate([cross, temporal], axis=-1)  2.34 us

profile of v2, /device:TPU:1, one launch (start us, length us, event | category | flops | bytes accessed | tf_op | source)
XLA Modules:
  0.0 72.9 jit_solution(16453391075697449892)
XLA Ops:
  0.0 70.5 %views_and_frames.1 = (bf16[3,128,768]{2,1,0:T(8,128)(2,1)}, bf16[3,128,768]{2,1,0:T(8,128)(2,1)}) custom-call(bf16[3,128,1536]{2,1,0:T(8,128)(2,1)} %q.1, bf16[3,128,1536]{2,1,0:T(8,128)(2,1)} %k.1, bf16[3,128,1536]{2,1,0:T(8,128)(2,1)} %v.1, s32[2,6]{1,0:T(2,128)} %bitcast.1), custom_call_target="tpu_custom_call" | custom-call | flops 3000000000 | bytes 5000000 | tf_op jit(solution)/shard_map/views_and_frames/pallas_call | solution.py:350
  70.5 2.3 %pad_maximum_fusion = bf16[3,128,1536]{2,1,0:T(8,128)(2,1)} fusion(bf16[3,128,768]{2,1,0:T(8,128)(2,1)} %get-tuple-element.8, bf16[3,128,768]{2,1,0:T(8,128)(2,1)} %get-tuple-element.7), kind=kLoop, calls=%fused_computation | loop fusion | flops 2359296 | bytes 2359296 | tf_op jit(solution)/shard_map/concatenate | solution.py:375

commit v3 on v2

--- a/solution.py
+++ b/solution.py
@@ -64,7 +64,7 @@
         pz = (z + dz) % RING
         return pz, (xl * 2 * RING + pz * 2 + core, tok)
 
-    peers = (1, 7, 2, 6, 3, 5, 4)
+    peers = (3, 5, 4, 2, 6, 1, 7)
     mine = pl.ds(core * CAMS, CAMS)
     cross_cols = pl.ds(0, HALF)
 
@@ -277,16 +277,16 @@
 
     last = []
     beside_send(0)
+    beside_send(1)
+    beside_send(2)
     own_send(0)
     start_own()
-    beside_send(1)
     own_send(1)
-    beside_send(2)
     own_send(2)
+    across_send(0)
+    across_send(1)
     pass_own()
     other_send(0)
-    across_send(0)
-    across_send(1)
     other_send(1)
     across_send(2)
     across_send(3)
@@ -297,30 +297,30 @@
     forward_x(1)
     temporal(0)
     pass_x(0)
+    forward_y(0)
     pass_x(1)
-    forward_y(0)
     forward_x(2)
     forward_y(1)
-    pass_y(0)
     temporal(1)
     forward_x(3)
+    pass_y(0)
     pass_x(2)
+    forward_y(2)
+    forward_x(4)
     pass_x(3)
-    forward_y(2)
     pass_y(1)
-    forward_x(4)
+    temporal(2)
+    forward_x(5)
+    forward_y(3)
+    pass_x(4)
     pass_y(2)
-    temporal(2)
-    pass_x(4)
-    forward_y(3)
-    forward_x(5)
+    relay(0)
+    forward_y(4)
     pass_x(5)
     pass_y(3)
-    relay(0)
-    forward_y(4)
-    pass_y(4)
     relay(1)
     forward_y(5)
+    pass_y(4)
     pass_y(5)
 
     for copy in to_across + sum(to_beside, []) + [*forwards.values(), *pairs_x.values(), *pairs_y.values()]:
@@ -368,7 +368,7 @@
             dma((3, 3)), dma((3, 3)), dma((3,)), dma((3,)), dma((3,)), dma((GROUPS,)),
         ],
         compiler_params=pltpu.CompilerParams(
-            collective_id=0, has_side_effects=True, vmem_limit_bytes=60 << 20),
+            collective_id=0, has_side_effects=True, vmem_limit_bytes=52 << 20),
         cost_estimate=pl.CostEstimate(flops=3_000_000_000, bytes_accessed=5_000_000, transcendentals=7_000_000),
         name="views_and_frames",
     )(queries, keys, values, adjacency.T)

time: 73 us -> 70.8 us (0.970)
  Pallas kernels: 70.5 us -> 68.9 us
  other arithmetic: 2.34 us -> 1.11 us
    pallas_call x1, Pallas kernels: 70.5 us -> 68.9 us  [body(): pl.pallas_call(kernel, out_shape=[jax.ShapeDtypeStruct((CAMS, ROWS, HALF)...]
    concatenate x1, other arithmetic: 2.34 us -> 1.11 us  [body(): return jnp.concatenate([cross, temporal], axis=-1)]
where the time goes in v3:
time: 70.8 us; the launch traced here: 70.7 us
  Pallas kernels  68.9 us (97%)
  other arithmetic  1.11 us (2%)
    pallas_call x1, Pallas kernels, body(): pl.pallas_call(kernel, out_shape=[jax.ShapeDtypeStruct((CAMS, ROWS, HALF)...  68.9 us

profile of v3, /device:TPU:1, one launch (start us, length us, event | category | flops | bytes accessed | tf_op | source)
XLA Modules:
  0.0 70.7 jit_solution(11373742654821291305)
XLA Ops:
  0.0 0.0 copy-start
  0.0 0.7 copy-done
  0.7 68.9 %views_and_frames.1 = (bf16[3,128,768]{2,1,0:T(8,128)(2,1)S(1)}, bf16[3,128,768]{2,1,0:T(8,128)(2,1)S(1)}) custom-call(bf16[3,128,1536]{2,1,0:T(8,128)(2,1)} %q.1, bf16[3,128,1536]{2,1,0:T(8,128)(2,1)} %k.1, bf16[3,128,1536]{2,1,0:T(8,128)(2,1)} %v.1, s32[2,6]{1,0:T(2,128)S(1)} %bitcast.1), custom_call_target="tpu_custom_call" | custom-call | flops 3000000000 | bytes 5000000 | tf_op jit(solution)/shard_map/views_and_frames/pallas_call | solution.py:350
  69.6 1.1 %pad_maximum_fusion = bf16[3,128,1536]{2,1,0:T(8,128)(2,1)} fusion(bf16[3,128,768]{2,1,0:T(8,128)(2,1)S(1)} %get-tuple-element.8, bf16[3,128,768]{2,1,0:T(8,128)(2,1)S(1)} %get-tuple-element.7), kind=kLoop, calls=%fused_computation | loop fusion | flops 2359296 | bytes 2359296 | tf_op jit(solution)/shard_map/concatenate | solution.py:375
Async XLA Ops:
  0.0 0.7 copy-start

commit v4 on v3

--- a/solution.py
+++ b/solution.py
@@ -276,10 +276,10 @@
         last[-1].start()
 
     last = []
+    own_send(0)
     beside_send(0)
     beside_send(1)
     beside_send(2)
-    own_send(0)
     start_own()
     own_send(1)
     own_send(2)

time: 70.8 us -> 71 us (level)
  no operation moved by 1% of the time
where the time goes in v4:
time: 71 us; the launch traced here: 70.9 us
  Pallas kernels  69.1 us (97%)
  other arithmetic  1.11 us (2%)
    pallas_call x1, Pallas kernels, body(): pl.pallas_call(kernel, out_shape=[jax.ShapeDtypeStruct((CAMS, ROWS, HALF)...  69.1 us

profile of v4, /device:TPU:1, one launch (start us, length us, event | category | flops | bytes accessed | tf_op | source)
XLA Modules:
  0.0 70.9 jit_solution(6692322411645586216)
XLA Ops:
  0.0 0.0 copy-start
  0.0 0.7 copy-done
  0.7 69.1 %views_and_frames.1 = (bf16[3,128,768]{2,1,0:T(8,128)(2,1)S(1)}, bf16[3,128,768]{2,1,0:T(8,128)(2,1)S(1)}) custom-call(bf16[3,128,1536]{2,1,0:T(8,128)(2,1)} %q.1, bf16[3,128,1536]{2,1,0:T(8,128)(2,1)} %k.1, bf16[3,128,1536]{2,1,0:T(8,128)(2,1)} %v.1, s32[2,6]{1,0:T(2,128)S(1)} %bitcast.1), custom_call_target="tpu_custom_call" | custom-call | flops 3000000000 | bytes 5000000 | tf_op jit(solution)/shard_map/views_and_frames/pallas_call | solution.py:350
  69.8 1.1 %pad_maximum_fusion = bf16[3,128,1536]{2,1,0:T(8,128)(2,1)} fusion(bf16[3,128,768]{2,1,0:T(8,128)(2,1)S(1)} %get-tuple-element.8, bf16[3,128,768]{2,1,0:T(8,128)(2,1)S(1)} %get-tuple-element.7), kind=kLoop, calls=%fused_computation | loop fusion | flops 2359296 | bytes 2359296 | tf_op jit(solution)/shard_map/concatenate | solution.py:375
Async XLA Ops:
  0.0 0.7 copy-start
